TPU v7x, 32 devices: a whole 2x2x4 slice. The times are simulated.
32 devices in a mesh: parts: 2 (over y), space: 4 (over z), src: 2 (over x), depth: 2 (over core).
Axes of the slice: x: 2, y: 2, z: 4, core: 2. Of those that a mesh axis runs over, the one named last changes fastest.
Arguments:
- start_fields: float32 [4, 3, 16, 128, 128], P(('parts', 'src'), None, 'space', 'depth'), parts along dimension 0, may hold values from -6 to 6
- adjoint_fields: float32 [4, 3, 16, 128, 128], P(('parts', 'src'), None, 'space', 'depth'), parts along dimension 0, may hold values from -6 to 6
- conductivity: float32 [32, 128, 128], P(('parts', 'space'), 'depth'), parts along dimension 0, may hold values from 0.02 to 0.5
- surface_rows: int32 [32, 128], P(('parts', 'space')), parts along dimension 0, may hold values from 0 to 16
- source_cells: int32 [4], P(('parts', 'src')), parts along dimension 0, may hold values from 0 to 262143
Outputs:
- fields: float32 [4, 3, 16, 128, 128], P(('parts', 'src'), None, 'space', 'depth'), parts along dimension 0
- gradient: float32 [32, 128, 128], P(('parts', 'space'), 'depth', 'src'), parts along dimension 0
There are 2 independent parts, one for each index of `parts`. A program takes and returns all parts, laid end to end along the dimension named above; each array names one. Nothing has to cross between parts.
Inputs may be any that keep to these rules, and one draw needn't show every extreme that they name: `source_cells`: flat cell index (x * 128 + z) * 128 + y. `surface_rows`: rows above it are air.
All inputs are finite; a program needn't handle non-finite values.
Results may differ from a plain program's by a relative error of at most 0.0001.
Values sent between devices are 32-bit elements; how exact they have to be, the bound alone decides.
A program may use at most 64 MiB of HBM per device.

v0:
```python
import jax
import jax.numpy as jnp
from jax import lax
from jax.sharding import PartitionSpec as P

ITERS = 3


ALPHA = 2.0
AIR = 0.01
SOURCE_AMP = 10.0


def with_halo(block, sides, width):
    for axis, dim in sides:
        count = lax.axis_size(axis)
        forward = [(i, i + 1) for i in range(count - 1)]
        backward = [(target, source) for source, target in forward]
        low = lax.ppermute(
            lax.slice_in_dim(block, block.shape[dim] - width, None, axis=dim), axis, forward
        )
        high = lax.ppermute(lax.slice_in_dim(block, 0, width, axis=dim), axis, backward)
        block = jnp.concatenate([low, block, high], axis=dim)
    return block


def curl_apply(padded, mass):
    e0 = padded[:, 0]
    e1 = padded[:, 1]
    e2 = padded[:, 2]

    def fwd_x(f):
        return f[:, 1:, :-1, :-1] - f[:, :-1, :-1, :-1]

    def fwd_z(f):
        return f[:, :-1, 1:, :-1] - f[:, :-1, :-1, :-1]

    def fwd_y(f):
        return f[:, :-1, :-1, 1:] - f[:, :-1, :-1, :-1]

    def back_x(h):
        return h[:, 1:, 1:, 1:] - h[:, :-1, 1:, 1:]

    def back_z(h):
        return h[:, 1:, 1:, 1:] - h[:, 1:, :-1, 1:]

    def back_y(h):
        return h[:, 1:, 1:, 1:] - h[:, 1:, 1:, :-1]

    curl_x = fwd_y(e2) - fwd_z(e1)
    curl_y = fwd_z(e0) - fwd_x(e2)
    curl_z = fwd_x(e1) - fwd_y(e0)
    out_x = back_y(curl_z) - back_z(curl_y)
    out_y = back_z(curl_x) - back_x(curl_z)
    out_z = back_x(curl_y) - back_y(curl_x)
    inner = padded[:, :, 1:-1, 1:-1, 1:-1]
    return jnp.stack((out_x, out_y, out_z), axis=1) + mass * inner


def column(vals):
    return vals[:, None, None, None, None]


def local_sum(left, right):
    return jnp.sum(left * right, axis=(1, 2, 3, 4))


def local(start_fields, adjoint_fields, conductivity, surface_rows, source_cells):
    cells_x = start_fields.shape[2]
    cells_z = start_fields.shape[3]
    cells_y = start_fields.shape[4]
    x_start = lax.axis_index("space") * cells_x
    z_start = lax.axis_index("depth") * cells_z
    depth_total = cells_z * lax.axis_size("depth")
    rows = z_start + jnp.arange(cells_z, dtype=jnp.int32)
    earth = rows[None, :, None] >= surface_rows[:, None, :]
    sigma = jnp.where(earth, conductivity, AIR)
    mass = ALPHA * sigma
    global_x = x_start + jnp.arange(cells_x, dtype=jnp.int32)
    flat = (global_x[:, None, None] * depth_total + rows[None, :, None]) * cells_y + jnp.arange(
        cells_y, dtype=jnp.int32
    )[None, None, :]
    onehot = jnp.where(flat[None] == source_cells[:, None, None, None], SOURCE_AMP, 0.0).astype(
        jnp.float32
    )
    blank = jnp.zeros_like(onehot)
    rhs = jnp.stack((onehot, blank, blank), axis=1)

    def apply(field):
        padded = with_halo(field, (("space", 2), ("depth", 3)), 1)
        padded = jnp.pad(padded, ((0, 0), (0, 0), (0, 0), (0, 0), (1, 1)))
        return curl_apply(padded, mass)

    x = start_fields
    r = rhs - apply(x)
    r0 = r
    rho = lax.psum(local_sum(r0, r), ("space", "depth"))
    p = r
    for step in range(ITERS):
        v = apply(p)
        alpha = rho / lax.psum(local_sum(r0, v), ("space", "depth"))
        s = r - column(alpha) * v
        t = apply(s)
        prod_ts, prod_tt = lax.psum((local_sum(t, s), local_sum(t, t)), ("space", "depth"))
        omega = prod_ts / prod_tt
        x = x + column(alpha) * p + column(omega) * s
        r = s - column(omega) * t
        if step + 1 < ITERS:
            rho_new = lax.psum(local_sum(r0, r), ("space", "depth"))
            beta = rho_new / rho * (alpha / omega)
            p = r + column(beta) * (p - column(omega) * v)
            rho = rho_new
    partial_total = jnp.sum(x * adjoint_fields, axis=(0, 1))
    summed = lax.psum_scatter(partial_total, "src", scatter_dimension=2, tiled=True)
    share = cells_y // lax.axis_size("src")
    offset = lax.axis_index("src") * share
    sigma_part = lax.dynamic_slice_in_dim(sigma, offset, share, 2)
    earth_part = lax.dynamic_slice_in_dim(earth, offset, share, 2)
    gradient = jnp.where(earth_part, -ALPHA * sigma_part * summed, 0.0)
    return (x, gradient)


def solution(mesh):
    placed = (
        P(("parts", "src"), None, "space", "depth", None),
        P(("parts", "src"), None, "space", "depth", None),
        P(("parts", "space"), "depth", None),
        P(("parts", "space"), None),
        P(("parts", "src")),
    )
    return jax.shard_map(
        local,
        mesh=mesh,
        in_specs=placed,
        out_specs=(
            P(("parts", "src"), None, "space", "depth", None),
            P(("parts", "space"), "depth", "src"),
        ),
        check_vma=False,
    )
```

profile of v0, /device:TPU:0, one launch (start us, length us, event | category | flops | bytes accessed | tf_op | source)
XLA Modules:
  0.0 268.7 jit_solution(16360025137695642032)
XLA Ops:
  8.2 4.9 %collective-permute-start = (f32[1,3,1,64,128]{4,3,2,1,0:T(8,128)S(1)}, f32[1,3,1,64,128]{4,3,2,1,0:T(8,128)S(1)}, u32[]{:S(2)}, u32[]{:S(2)}) collective-permute-start(f32[1,3,1,64,128]{4,3,2,1,0:T(8,128)S(1)} %get-tuple-element.93), channel_id=1, source_target_pairs={{0,4},{4,8},{8,12},{1,5},{5,9},{9,13},{2,6},{6,10},{10,14},{3,7},{... | collective-permute-start | bytes 294920 | tf_op jit(solution)/shard_map/ppermute | solution.py:19
  14.4 1.7 broadcast_multiply_fusion
  17.9 1.7 collective-permute-done.1
  22.4 1.7 collective-permute-done.3
  26.0 3.5 %collective-permute-start.4 = (f32[1,3,1,64,128]{4,3,2,1,0:T(8,128)S(1)}, f32[1,3,1,64,128]{4,3,2,1,0:T(8,128)S(1)}, u32[]{:S(2)}, u32[]{:S(2)}) collective-permute-start(f32[1,3,1,64,128]{4,3,2,1,0:T(8,128)S(1)} %get-tuple-element.90), channel_id=1, source_target_pairs={{0,4},{4,8},{8,12},{1,5},{5,9},{9,13},{2,6},{6,10},{10,14},{3,7},{... | collective-permute-start | bytes 294920 | tf_op jit(solution)/shard_map/ppermute | solution.py:19
  31.8 4.1 %collective-permute-done.5 = f32[1,3,1,64,128]{4,3,2,1,0:T(8,128)S(1)} collective-permute-done((f32[1,3,1,64,128]{4,3,2,1,0:T(8,128)S(1)}, f32[1,3,1,64,128]{4,3,2,1,0:T(8,128)S(1)}, u32[]{:S(2)}, u32[]{:S(2)}) %collective-permute-start.5) | collective-permute-done | bytes 98336 | tf_op jit(solution)/shard_map/ppermute | solution.py:22
  38.6 1.8 collective-permute-done.7
  42.4 15.0 %all-reduce.11 = (f32[1]{0:T(128)}, f32[1]{0:T(128)}) all-reduce(f32[1]{0:T(128)} %bitcast.9, f32[1]{0:T(128)} %bitcast.16), channel_id=1, replica_groups=mesh['parts'=2,'space'=4,'src'=2,'depth'=2] {'space','depth'}, use_global_device_ids=true, to_apply=%region_1.2 | all-reduce | flops 2 | bytes 16 | tf_op jit(solution)/shard_map/psum | solution.py:97
  58.8 1.3 collective-permute-start.8
  62.3 4.3 %collective-permute-done.9 = f32[1,3,1,64,128]{4,3,2,1,0:T(8,128)S(1)} collective-permute-done((f32[1,3,1,64,128]{4,3,2,1,0:T(8,128)S(1)}, f32[1,3,1,64,128]{4,3,2,1,0:T(8,128)S(1)}, u32[]{:S(2)}, u32[]{:S(2)}) %collective-permute-start.9) | collective-permute-done | bytes 98336 | tf_op jit(solution)/shard_map/ppermute | solution.py:22
  69.3 1.8 collective-permute-done.11
  73.1 14.4 %all-reduce.10 = (f32[1]{0:T(128)}, f32[1]{0:T(128)}) all-reduce(f32[1]{0:T(128)} %bitcast.24, f32[1]{0:T(128)} %bitcast.25), channel_id=1, replica_groups=mesh['parts'=2,'space'=4,'src'=2,'depth'=2] {'space','depth'}, use_global_device_ids=true, to_apply=%region_5.6 | all-reduce | flops 2 | bytes 16 | tf_op jit(solution)/shard_map/psum | solution.py:104
  92.0 14.2 %psum.88 = f32[1]{0:T(128)} all-reduce(f32[1]{0:T(128)} %bitcast.27), channel_id=1, replica_groups=mesh['parts'=2,'space'=4,'src'=2,'depth'=2] {'space','depth'}, use_global_device_ids=true, to_apply=%region_9.10 | all-reduce | flops 1 | bytes 8 | tf_op jit(solution)/shard_map/psum | solution.py:109
  107.7 1.3 collective-permute-start.12
  111.3 4.1 %collective-permute-done.13 = f32[1,3,1,64,128]{4,3,2,1,0:T(8,128)S(1)} collective-permute-done((f32[1,3,1,64,128]{4,3,2,1,0:T(8,128)S(1)}, f32[1,3,1,64,128]{4,3,2,1,0:T(8,128)S(1)}, u32[]{:S(2)}, u32[]{:S(2)}) %collective-permute-start.13) | collective-permute-done | bytes 98336 | tf_op jit(solution)/shard_map/ppermute | solution.py:22
  118.1 1.8 collective-permute-done.15
  121.8 14.4 %psum.89 = f32[1]{0:T(128)} all-reduce(f32[1]{0:T(128)} %bitcast.35), channel_id=1, replica_groups=mesh['parts'=2,'space'=4,'src'=2,'depth'=2] {'space','depth'}, use_global_device_ids=true, to_apply=%region_11.12 | all-reduce | flops 1 | bytes 8 | tf_op jit(solution)/shard_map/psum | solution.py:101
  137.9 1.3 collective-permute-start.16
  141.4 4.3 %collective-permute-done.17 = f32[1,3,1,64,128]{4,3,2,1,0:T(8,128)S(1)} collective-permute-done((f32[1,3,1,64,128]{4,3,2,1,0:T(8,128)S(1)}, f32[1,3,1,64,128]{4,3,2,1,0:T(8,128)S(1)}, u32[]{:S(2)}, u32[]{:S(2)}) %collective-permute-start.17) | collective-permute-done | bytes 98336 | tf_op jit(solution)/shard_map/ppermute | solution.py:22
  148.4 1.8 collective-permute-done.19
  152.1 14.4 %all-reduce.9 = (f32[1]{0:T(128)}, f32[1]{0:T(128)}) all-reduce(f32[1]{0:T(128)} %bitcast.43, f32[1]{0:T(128)} %bitcast.44), channel_id=1, replica_groups=mesh['parts'=2,'space'=4,'src'=2,'depth'=2] {'space','depth'}, use_global_device_ids=true, to_apply=%region_13.14 | all-reduce | flops 2 | bytes 16 | tf_op jit(solution)/shard_map/psum | solution.py:104
  171.2 14.3 %psum.92 = f32[1]{0:T(128)} all-reduce(f32[1]{0:T(128)} %bitcast.46), channel_id=1, replica_groups=mesh['parts'=2,'space'=4,'src'=2,'depth'=2] {'space','depth'}, use_global_device_ids=true, to_apply=%region_17.18 | all-reduce | flops 1 | bytes 8 | tf_op jit(solution)/shard_map/psum | solution.py:109
  190.6 4.1 %collective-permute-done.21 = f32[1,3,1,64,128]{4,3,2,1,0:T(8,128)S(1)} collective-permute-done((f32[1,3,1,64,128]{4,3,2,1,0:T(8,128)S(1)}, f32[1,3,1,64,128]{4,3,2,1,0:T(8,128)S(1)}, u32[]{:S(2)}, u32[]{:S(2)}) %collective-permute-start.21) | collective-permute-done | bytes 98336 | tf_op jit(solution)/shard_map/ppermute | solution.py:22
  196.0 1.5 collective-permute-start.23
  197.5 1.6 collective-permute-done.23
  201.7 14.4 %psum.93 = f32[1]{0:T(128)} all-reduce(f32[1]{0:T(128)} %bitcast.54), channel_id=1, replica_groups=mesh['parts'=2,'space'=4,'src'=2,'depth'=2] {'space','depth'}, use_global_device_ids=true, to_apply=%region_19.20 | all-reduce | flops 1 | bytes 8 | tf_op jit(solution)/shard_map/psum | solution.py:101
  218.4 1.3 collective-permute-start.24
  221.9 4.3 %collective-permute-done.25 = f32[1,3,1,64,128]{4,3,2,1,0:T(8,128)S(1)} collective-permute-done((f32[1,3,1,64,128]{4,3,2,1,0:T(8,128)S(1)}, f32[1,3,1,64,128]{4,3,2,1,0:T(8,128)S(1)}, u32[]{:S(2)}, u32[]{:S(2)}) %collective-permute-start.25) | collective-permute-done | bytes 98336 | tf_op jit(solution)/shard_map/ppermute | solution.py:22
  228.8 1.8 collective-permute-done.27
  232.5 14.4 %all-reduce.8 = (f32[1]{0:T(128)}, f32[1]{0:T(128)}) all-reduce(f32[1]{0:T(128)} %bitcast.62, f32[1]{0:T(128)} %bitcast.63), channel_id=1, replica_groups=mesh['parts'=2,'space'=4,'src'=2,'depth'=2] {'space','depth'}, use_global_device_ids=true, to_apply=%region_21.22 | all-reduce | flops 2 | bytes 16 | tf_op jit(solution)/shard_map/psum | solution.py:104
  248.2 2.1 multiply_reduce_fusion
  251.5 8.5 %reduce-scatter.4.cloned.1.call-done = f32[64,256]{1,0:T(8,128)} async-done(((f32[128,256]{1,0:T(8,128)}), f32[64,256]{1,0:T(8,128)}) %reduce-scatter.4.cloned.1.call-update) | async-done | bytes 65552
  (124 shorter events, 56.1 us)
Async XLA Ops:
  7.2 252.8 %reduce-scatter.4.cloned.1.call-start = ((), (), s32[]{:S(2)}) async-start(), calls=%async_computation.1 | async-start | bytes 196608
  8.2 8.7 %collective-permute-start = (f32[1,3,1,64,128]{4,3,2,1,0:T(8,128)S(1)}, f32[1,3,1,64,128]{4,3,2,1,0:T(8,128)S(1)}, u32[]{:S(2)}, u32[]{:S(2)}) collective-permute-start(f32[1,3,1,64,128]{4,3,2,1,0:T(8,128)S(1)} %get-tuple-element.93), channel_id=1, source_target_pairs={{0,4},{4,8},{8,12},{1,5},{5,9},{9,13},{2,6},{6,10},{10,14},{3,7},{... | collective-permute-start | bytes 294920 | tf_op jit(solution)/shard_map/ppermute | solution.py:19
  13.1 6.5 %collective-permute-start.1 = (f32[1,3,1,64,128]{4,3,2,1,0:T(8,128)S(1)}, f32[1,3,1,64,128]{4,3,2,1,0:T(8,128)S(1)}, u32[]{:S(2)}, u32[]{:S(2)}) collective-permute-start(f32[1,3,1,64,128]{4,3,2,1,0:T(8,128)S(1)} %get-tuple-element.92), channel_id=1, source_target_pairs={{4,0},{8,4},{12,8},{5,1},{9,5},{13,9},{6,2},{10,6},{14,10},{7,3},{... | collective-permute-start | bytes 294920 | tf_op jit(solution)/shard_map/ppermute | solution.py:22
  19.7 2.7 %collective-permute-start.2 = (f32[1,3,6,1,128]{4,3,2,1,0:T(1,128)S(1)}, f32[1,3,6,1,128]{4,3,2,1,0:T(1,128)S(1)}, u32[]{:S(2)}, u32[]{:S(2)}) collective-permute-start(f32[1,3,6,1,128]{4,3,2,1,0:T(1,128)S(1)} %get-tuple-element.57), channel_id=1, source_target_pairs={{0,1},{2,3},{4,5},{6,7},{8,9},{10,11},{12,13},{14,15},{16,17},{18,... | collective-permute-start | bytes 27656 | tf_op jit(solution)/shard_map/ppermute | solution.py:19
  21.0 3.1 %collective-permute-start.3 = (f32[1,3,6,1,128]{4,3,2,1,0:T(1,128)S(1)}, f32[1,3,6,1,128]{4,3,2,1,0:T(1,128)S(1)}, u32[]{:S(2)}, u32[]{:S(2)}) collective-permute-start(f32[1,3,6,1,128]{4,3,2,1,0:T(1,128)S(1)} %get-tuple-element.58), channel_id=1, source_target_pairs={{1,0},{3,2},{5,4},{7,6},{9,8},{11,10},{13,12},{15,14},{17,16},{19,... | collective-permute-start | bytes 27656 | tf_op jit(solution)/shard_map/ppermute | solution.py:22
  26.0 5.9 %collective-permute-start.4 = (f32[1,3,1,64,128]{4,3,2,1,0:T(8,128)S(1)}, f32[1,3,1,64,128]{4,3,2,1,0:T(8,128)S(1)}, u32[]{:S(2)}, u32[]{:S(2)}) collective-permute-start(f32[1,3,1,64,128]{4,3,2,1,0:T(8,128)S(1)} %get-tuple-element.90), channel_id=1, source_target_pairs={{0,4},{4,8},{8,12},{1,5},{5,9},{9,13},{2,6},{6,10},{10,14},{3,7},{... | collective-permute-start | bytes 294920 | tf_op jit(solution)/shard_map/ppermute | solution.py:19
  29.5 6.5 %collective-permute-start.5 = (f32[1,3,1,64,128]{4,3,2,1,0:T(8,128)S(1)}, f32[1,3,1,64,128]{4,3,2,1,0:T(8,128)S(1)}, u32[]{:S(2)}, u32[]{:S(2)}) collective-permute-start(f32[1,3,1,64,128]{4,3,2,1,0:T(8,128)S(1)} %get-tuple-element.91), channel_id=1, source_target_pairs={{4,0},{8,4},{12,8},{5,1},{9,5},{13,9},{6,2},{10,6},{14,10},{7,3},{... | collective-permute-start | bytes 294920 | tf_op jit(solution)/shard_map/ppermute | solution.py:22
  36.0 2.6 collective-permute-start.6
  37.3 3.1 %collective-permute-start.7 = (f32[1,3,6,1,128]{4,3,2,1,0:T(1,128)S(1)}, f32[1,3,6,1,128]{4,3,2,1,0:T(1,128)S(1)}, u32[]{:S(2)}, u32[]{:S(2)}) collective-permute-start(f32[1,3,6,1,128]{4,3,2,1,0:T(1,128)S(1)} %get-tuple-element.56), channel_id=1, source_target_pairs={{1,0},{3,2},{5,4},{7,6},{9,8},{11,10},{13,12},{15,14},{17,16},{19,... | collective-permute-start | bytes 27656 | tf_op jit(solution)/shard_map/ppermute | solution.py:22
  58.8 3.5 %collective-permute-start.8 = (f32[1,3,1,64,128]{4,3,2,1,0:T(8,128)S(1)}, f32[1,3,1,64,128]{4,3,2,1,0:T(8,128)S(1)}, u32[]{:S(2)}, u32[]{:S(2)}) collective-permute-start(f32[1,3,1,64,128]{4,3,2,1,0:T(8,128)S(1)} %get-tuple-element.88), channel_id=1, source_target_pairs={{0,4},{4,8},{8,12},{1,5},{5,9},{9,13},{2,6},{6,10},{10,14},{3,7},{... | collective-permute-start | bytes 294920 | tf_op jit(solution)/shard_map/ppermute | solution.py:19
  60.1 6.5 %collective-permute-start.9 = (f32[1,3,1,64,128]{4,3,2,1,0:T(8,128)S(1)}, f32[1,3,1,64,128]{4,3,2,1,0:T(8,128)S(1)}, u32[]{:S(2)}, u32[]{:S(2)}) collective-permute-start(f32[1,3,1,64,128]{4,3,2,1,0:T(8,128)S(1)} %get-tuple-element.89), channel_id=1, source_target_pairs={{4,0},{8,4},{12,8},{5,1},{9,5},{13,9},{6,2},{10,6},{14,10},{7,3},{... | collective-permute-start | bytes 294920 | tf_op jit(solution)/shard_map/ppermute | solution.py:22
  66.6 2.6 collective-permute-start.10
  67.9 3.1 %collective-permute-start.11 = (f32[1,3,6,1,128]{4,3,2,1,0:T(1,128)S(1)}, f32[1,3,6,1,128]{4,3,2,1,0:T(1,128)S(1)}, u32[]{:S(2)}, u32[]{:S(2)}) collective-permute-start(f32[1,3,6,1,128]{4,3,2,1,0:T(1,128)S(1)} %get-tuple-element.54), channel_id=1, source_target_pairs={{1,0},{3,2},{5,4},{7,6},{9,8},{11,10},{13,12},{15,14},{17,16},{19,... | collective-permute-start | bytes 27656 | tf_op jit(solution)/shard_map/ppermute | solution.py:22
  107.7 3.7 %collective-permute-start.12 = (f32[1,3,1,64,128]{4,3,2,1,0:T(8,128)S(1)}, f32[1,3,1,64,128]{4,3,2,1,0:T(8,128)S(1)}, u32[]{:S(2)}, u32[]{:S(2)}) collective-permute-start(f32[1,3,1,64,128]{4,3,2,1,0:T(8,128)S(1)} %get-tuple-element.86), channel_id=1, source_target_pairs={{0,4},{4,8},{8,12},{1,5},{5,9},{9,13},{2,6},{6,10},{10,14},{3,7},{... | collective-permute-start | bytes 294920 | tf_op jit(solution)/shard_map/ppermute | solution.py:19
  109.0 6.5 %collective-permute-start.13 = (f32[1,3,1,64,128]{4,3,2,1,0:T(8,128)S(1)}, f32[1,3,1,64,128]{4,3,2,1,0:T(8,128)S(1)}, u32[]{:S(2)}, u32[]{:S(2)}) collective-permute-start(f32[1,3,1,64,128]{4,3,2,1,0:T(8,128)S(1)} %get-tuple-element.87), channel_id=1, source_target_pairs={{4,0},{8,4},{12,8},{5,1},{9,5},{13,9},{6,2},{10,6},{14,10},{7,3},{... | collective-permute-start | bytes 294920 | tf_op jit(solution)/shard_map/ppermute | solution.py:22
  115.5 2.6 collective-permute-start.14
  116.8 3.1 %collective-permute-start.15 = (f32[1,3,6,1,128]{4,3,2,1,0:T(1,128)S(1)}, f32[1,3,6,1,128]{4,3,2,1,0:T(1,128)S(1)}, u32[]{:S(2)}, u32[]{:S(2)}) collective-permute-start(f32[1,3,6,1,128]{4,3,2,1,0:T(1,128)S(1)} %get-tuple-element.52), channel_id=1, source_target_pairs={{1,0},{3,2},{5,4},{7,6},{9,8},{11,10},{13,12},{15,14},{17,16},{19,... | collective-permute-start | bytes 27656 | tf_op jit(solution)/shard_map/ppermute | solution.py:22
  121.0 16.8 %copy-start.1 = (f32[1,1,4,64,128]{4,3,2,1,0:T(8,128)}, f32[1,1,4,64,128]{4,3,2,1,0:T(8,128)S(1)}, u32[]{:S(2)}) copy-start(f32[1,1,4,64,128]{4,3,2,1,0:T(8,128)S(1)} %get-tuple-element.104) | copy-start | bytes 393220
  137.9 3.5 %collective-permute-start.16 = (f32[1,3,1,64,128]{4,3,2,1,0:T(8,128)S(1)}, f32[1,3,1,64,128]{4,3,2,1,0:T(8,128)S(1)}, u32[]{:S(2)}, u32[]{:S(2)}) collective-permute-start(f32[1,3,1,64,128]{4,3,2,1,0:T(8,128)S(1)} %get-tuple-element.84), channel_id=1, source_target_pairs={{0,4},{4,8},{8,12},{1,5},{5,9},{9,13},{2,6},{6,10},{10,14},{3,7},{... | collective-permute-start | bytes 294920 | tf_op jit(solution)/shard_map/ppermute | solution.py:19
  139.2 6.5 %collective-permute-start.17 = (f32[1,3,1,64,128]{4,3,2,1,0:T(8,128)S(1)}, f32[1,3,1,64,128]{4,3,2,1,0:T(8,128)S(1)}, u32[]{:S(2)}, u32[]{:S(2)}) collective-permute-start(f32[1,3,1,64,128]{4,3,2,1,0:T(8,128)S(1)} %get-tuple-element.85), channel_id=1, source_target_pairs={{4,0},{8,4},{12,8},{5,1},{9,5},{13,9},{6,2},{10,6},{14,10},{7,3},{... | collective-permute-start | bytes 294920 | tf_op jit(solution)/shard_map/ppermute | solution.py:22
  145.8 2.6 collective-permute-start.18
  147.1 3.1 %collective-permute-start.19 = (f32[1,3,6,1,128]{4,3,2,1,0:T(1,128)S(1)}, f32[1,3,6,1,128]{4,3,2,1,0:T(1,128)S(1)}, u32[]{:S(2)}, u32[]{:S(2)}) collective-permute-start(f32[1,3,6,1,128]{4,3,2,1,0:T(1,128)S(1)} %get-tuple-element.50), channel_id=1, source_target_pairs={{1,0},{3,2},{5,4},{7,6},{9,8},{11,10},{13,12},{15,14},{17,16},{19,... | collective-permute-start | bytes 27656 | tf_op jit(solution)/shard_map/ppermute | solution.py:22
  152.1 34.6 %copy-start.2 = (f32[1,1,4,64,128]{4,3,2,1,0:T(8,128)S(1)}, f32[1,1,4,64,128]{4,3,2,1,0:T(8,128)}, u32[]{:S(2)}) copy-start(f32[1,1,4,64,128]{4,3,2,1,0:T(8,128)} %copy-done.1) | copy-start | bytes 393220
  152.1 34.6 %copy-start.4 = (f32[1,1,4,64,128]{4,3,2,1,0:T(8,128)S(1)}, f32[1,1,4,64,128]{4,3,2,1,0:T(8,128)}, u32[]{:S(2)}) copy-start(f32[1,1,4,64,128]{4,3,2,1,0:T(8,128)} %copy-done.3) | copy-start | bytes 393220
  186.9 3.7 %collective-permute-start.20 = (f32[1,3,1,64,128]{4,3,2,1,0:T(8,128)S(1)}, f32[1,3,1,64,128]{4,3,2,1,0:T(8,128)S(1)}, u32[]{:S(2)}, u32[]{:S(2)}) collective-permute-start(f32[1,3,1,64,128]{4,3,2,1,0:T(8,128)S(1)} %get-tuple-element.82), channel_id=1, source_target_pairs={{0,4},{4,8},{8,12},{1,5},{5,9},{9,13},{2,6},{6,10},{10,14},{3,7},{... | collective-permute-start | bytes 294920 | tf_op jit(solution)/shard_map/ppermute | solution.py:19
  188.2 6.5 %collective-permute-start.21 = (f32[1,3,1,64,128]{4,3,2,1,0:T(8,128)S(1)}, f32[1,3,1,64,128]{4,3,2,1,0:T(8,128)S(1)}, u32[]{:S(2)}, u32[]{:S(2)}) collective-permute-start(f32[1,3,1,64,128]{4,3,2,1,0:T(8,128)S(1)} %get-tuple-element.83), channel_id=1, source_target_pairs={{4,0},{8,4},{12,8},{5,1},{9,5},{13,9},{6,2},{10,6},{14,10},{7,3},{... | collective-permute-start | bytes 294920 | tf_op jit(solution)/shard_map/ppermute | solution.py:22
  194.7 2.8 %collective-permute-start.22 = (f32[1,3,6,1,128]{4,3,2,1,0:T(1,128)S(1)}, f32[1,3,6,1,128]{4,3,2,1,0:T(1,128)S(1)}, u32[]{:S(2)}, u32[]{:S(2)}) collective-permute-start(f32[1,3,6,1,128]{4,3,2,1,0:T(1,128)S(1)} %get-tuple-element.47), channel_id=1, source_target_pairs={{0,1},{2,3},{4,5},{6,7},{8,9},{10,11},{12,13},{14,15},{16,17},{18,... | collective-permute-start | bytes 27656 | tf_op jit(solution)/shard_map/ppermute | solution.py:19
  196.0 3.1 %collective-permute-start.23 = (f32[1,3,6,1,128]{4,3,2,1,0:T(1,128)S(1)}, f32[1,3,6,1,128]{4,3,2,1,0:T(1,128)S(1)}, u32[]{:S(2)}, u32[]{:S(2)}) collective-permute-start(f32[1,3,6,1,128]{4,3,2,1,0:T(1,128)S(1)} %get-tuple-element.48), channel_id=1, source_target_pairs={{1,0},{3,2},{5,4},{7,6},{9,8},{11,10},{13,12},{15,14},{17,16},{19,... | collective-permute-start | bytes 27656 | tf_op jit(solution)/shard_map/ppermute | solution.py:22
  218.4 3.5 %collective-permute-start.24 = (f32[1,3,1,64,128]{4,3,2,1,0:T(8,128)S(1)}, f32[1,3,1,64,128]{4,3,2,1,0:T(8,128)S(1)}, u32[]{:S(2)}, u32[]{:S(2)}) collective-permute-start(f32[1,3,1,64,128]{4,3,2,1,0:T(8,128)S(1)} %get-tuple-element.80), channel_id=1, source_target_pairs={{0,4},{4,8},{8,12},{1,5},{5,9},{9,13},{2,6},{6,10},{10,14},{3,7},{... | collective-permute-start | bytes 294920 | tf_op jit(solution)/shard_map/ppermute | solution.py:19
  219.7 6.5 %collective-permute-start.25 = (f32[1,3,1,64,128]{4,3,2,1,0:T(8,128)S(1)}, f32[1,3,1,64,128]{4,3,2,1,0:T(8,128)S(1)}, u32[]{:S(2)}, u32[]{:S(2)}) collective-permute-start(f32[1,3,1,64,128]{4,3,2,1,0:T(8,128)S(1)} %get-tuple-element.81), channel_id=1, source_target_pairs={{4,0},{8,4},{12,8},{5,1},{9,5},{13,9},{6,2},{10,6},{14,10},{7,3},{... | collective-permute-start | bytes 294920 | tf_op jit(solution)/shard_map/ppermute | solution.py:22
  226.2 2.6 collective-permute-start.26
  227.5 3.1 %collective-permute-start.27 = (f32[1,3,6,1,128]{4,3,2,1,0:T(1,128)S(1)}, f32[1,3,6,1,128]{4,3,2,1,0:T(1,128)S(1)}, u32[]{:S(2)}, u32[]{:S(2)}) collective-permute-start(f32[1,3,6,1,128]{4,3,2,1,0:T(1,128)S(1)} %get-tuple-element.46), channel_id=1, source_target_pairs={{1,0},{3,2},{5,4},{7,6},{9,8},{11,10},{13,12},{15,14},{17,16},{19,... | collective-permute-start | bytes 27656 | tf_op jit(solution)/shard_map/ppermute | solution.py:22
  (6 other events, 33.8 us)
Sparse Core Ops, SparseCore 0:
  251.5 8.4 reduce-scatter.3
where the time goes:
time: 270 us; the launch traced here: 269 us
  blocking collectives  115 us (43%)
  waiting for transfers between devices  53.6 us (20%)
  starting transfers between devices  42.2 us (16%)
  between operations  30.6 us (11%)
  other arithmetic  20.7 us (8%)
  local copies, waits for them, and re-layouts  6.11 us (2%)
    psum x3, blocking collectives, local(): lax.psum((local_sum(t, s), local_sum(t, t)), ('space', 'depth'))  43.2 us
    ppermute x14, waiting for transfers between devices, with_halo(): lax.ppermute(lax.slice_in_dim(block, 0, width, axis=dim), axis, backward)  39.2 us
    psum x2, blocking collectives, local(): alpha = rho / lax.psum(local_sum(r0, v), ('space', 'depth'))  28.8 us
    psum x2, blocking collectives, local(): rho_new = lax.psum(local_sum(r0, r), ('space', 'depth'))  28.5 us
    ppermute x14, starting transfers between devices, with_halo(): lax.ppermute(lax.slice_in_dim(block, block.shape[dim] - width, None, axis...  23.9 us
    ppermute x14, starting transfers between devices, with_halo(): lax.ppermute(lax.slice_in_dim(block, 0, width, axis=dim), axis, backward)  18.3 us
    psum x1, blocking collectives, local(): rho = lax.psum(local_sum(r0, r), ('space', 'depth'))  15 us
    unnamed x2, waiting for transfers between devices  8.52 us
  transfers between devices with their start and end apart: 29, of which 21 were waited for; matrix products, arithmetic and copies ran while one was open for 1% of the time, Pallas kernels for 0%

commit v1 on v0

v1 whole, which is shorter than its diff:
```python
import functools

import jax
import jax.numpy as jnp
from jax import lax
from jax.experimental import pallas as pl
from jax.experimental.pallas import tpu as pltpu
from jax.sharding import PartitionSpec as P

ITERS = 3
ALPHA = 2.0
AIR = 0.01
SOURCE_AMP = 10.0
CENTRE = 6.5
HALF = 6.5
DEGREE = 2 * ITERS
APPLIES = DEGREE + 1
PAD = 8
MESH = pl.DeviceIdType.MESH


def times_operator(poly):
    out = [None] * (len(poly) + 1)

    def add(k, term):
        out[k] = term if out[k] is None else out[k] + term

    for k, c in enumerate(poly):
        add(k, CENTRE * c)
        if k == 0:
            add(1, HALF * c)
        else:
            add(k + 1, (0.5 * HALF) * c)
            add(k - 1, (0.5 * HALF) * c)
    return out


def axpy(a, scale, b):
    out = []
    for k in range(max(len(a), len(b))):
        if k >= len(b):
            out.append(a[k])
        elif k >= len(a):
            out.append(scale * b[k])
        else:
            out.append(a[k] + scale * b[k])
    return out


def with_first(poly, moments):
    total = poly[0] * moments[0]
    for k in range(1, len(poly)):
        total = total + poly[k] * moments[k]
    return total


def inner(a, b, moments):
    total = None
    for i, u in enumerate(a):
        row = None
        for j, w in enumerate(b):
            term = w * (0.5 * (moments[i + j] + moments[abs(i - j)]))
            row = term if row is None else row + term
        total = u * row if total is None else total + u * row
    return total


def field_coefficients(moments):
    one = jnp.ones_like(moments[0])
    r = [one]
    p = [one]
    rho = moments[0]
    x = []
    for step in range(ITERS):
        v = times_operator(p)
        alpha = rho / with_first(v, moments)
        s = axpy(r, -alpha, v)
        t = times_operator(s)
        omega = inner(t, s, moments) / inner(t, t, moments)
        x = axpy(axpy(x, alpha, p), omega, s)
        if step + 1 < ITERS:
            r = axpy(s, -omega, t)
            rho_new = with_first(r, moments)
            beta = rho_new / rho * (alpha / omega)
            p = axpy(r, beta, axpy(p, -omega, v))
            rho = rho_new
    return x


def kernel(
    sizes,
    start_ref,
    adj_ref,
    cond_ref,
    surf_ref,
    cell_ref,
    out_ref,
    grad_ref,
    basis,
    right_in,
    left_in,
    left_out,
    rows_out,
    rows_in,
    mass,
    dots,
    dots_out,
    dots_in,
    share_out,
    share_in,
    load_sem,
    send_sem,
    recv_sem,
    dot_send,
    dot_recv,
    share_send,
    share_recv,
):
    n_space, n_src, cx, cz, cy = sizes
    group = n_space * 2
    share = cy // n_src
    last = cx - 1
    s = lax.axis_index("space")
    d = lax.axis_index("depth")
    c = lax.axis_index("src")
    me = s * 2 + d

    def member(k):
        g = lax.rem(me + k, group)
        return {"space": g // 2, "depth": lax.rem(g, 2)}

    def source(k):
        return {"src": lax.rem(c + k, n_src)}

    barrier = pltpu.get_barrier_semaphore()

    def greet(k, carry):
        pl.semaphore_signal(barrier, inc=1, device_id=member(k), device_id_type=MESH)
        return carry

    lax.fori_loop(1, group, greet, 0)
    for k in range(1, n_src):
        pl.semaphore_signal(barrier, inc=1, device_id=source(k), device_id_type=MESH)

    own = pl.ds(PAD, cz)
    load = pltpu.make_async_copy(start_ref.at[0], basis.at[0, :, :, own, :], load_sem)
    load.start()

    lane = lax.broadcasted_iota(jnp.int32, (cz, cy), 1)
    row = lax.broadcasted_iota(jnp.int32, (cz, cy), 0)
    first_lane = lane == 0
    last_lane = lane == cy - 1
    z_start = d * cz
    zero_row = jnp.zeros((1, cy), jnp.float32)

    def earth(x):
        return (z_start + row) >= surf_ref[pl.ds(x, 1), :]

    for x in range(cx):
        mass[x] = ALPHA * jnp.where(earth(x), cond_ref[x], AIR)
    zero_rows = jnp.zeros((3, cx, 1, cy), jnp.float32)

    def clear(j, carry):
        basis[j, :, :, PAD - 1 : PAD, :] = zero_rows
        basis[j, :, :, PAD + cz : PAD + cz + 1, :] = zero_rows
        right_in[j, 1, PAD - 1 : PAD, :] = zero_row
        rows_out[j] = jnp.zeros((16, cy), jnp.float32)
        return carry

    lax.fori_loop(0, APPLIES, clear, 0)

    @pl.when(s == 0)
    def _():
        left_in[...] = jnp.zeros(left_in.shape, jnp.float32)

    @pl.when(s == n_space - 1)
    def _():
        def blank(j, carry):
            right_in[j, :, own, :] = jnp.zeros((2, cz, cy), jnp.float32)
            return carry

        lax.fori_loop(0, APPLIES, blank, 0)

    def before(f):
        return jnp.where(first_lane, 0.0, pltpu.roll(f, 1, 1))

    def after(f):
        return jnp.where(last_lane, 0.0, pltpu.roll(f, cy - 1, 1))

    def copy(j, kind):
        if kind == 0:
            src, dst, where = left_out.at[j], left_in.at[j], {"space": s + 1}
        elif kind == 1:
            src = basis.at[j, pl.ds(1, 2), 0, own, :]
            dst, where = right_in.at[j, :, own, :], {"space": s - 1}
        else:
            src, dst = rows_out.at[j], rows_in.at[j, kind - 2]
            where = {"depth": 1 - d}
            if kind == 3:
                where["space"] = s + 1
            elif kind == 4:
                where["space"] = s - 1
        return pltpu.make_async_remote_copy(
            src_ref=src,
            dst_ref=dst,
            send_sem=send_sem.at[j, kind],
            recv_sem=recv_sem.at[j, kind],
            device_id=where,
            device_id_type=MESH,
        )

    has_left = s > 0
    has_right = s < n_space - 1

    def send_right(j):
        e0 = basis[j, 0, last, own, :]
        left_out[j, 0] = basis[j, 1, last, own, :] + after(e0) - e0
        left_out[j, 1] = basis[j, 2, last, own, :] + basis[j, 0, last, pl.ds(PAD + 1, cz), :] - e0

        @pl.when(has_right)
        def _():
            copy(j, 0).start()

    def send_left(j):
        @pl.when(has_left)
        def _():
            copy(j, 1).start()

    edge = PAD + (cz - 1) * (1 - d)

    def send_rows(j):
        for q in range(3):
            for x in range(cx):
                rows_out[j, q * cx + x : q * cx + x + 1, :] = basis[j, q, x, pl.ds(edge, 1), :]
        copy(j, 2).start()

        @pl.when(has_right)
        def _():
            copy(j, 3).start()

        @pl.when(has_left)
        def _():
            copy(j, 4).start()

    def take_rows(j):
        copy(j, 2).wait_recv()
        target = PAD - 1 + (cz + 1) * (1 - d)
        for q in range(3):
            for x in range(cx):
                basis[j, q, x, pl.ds(target, 1), :] = rows_in[j, 0, q * cx + x : q * cx + x + 1, :]

    def take_sides(j):
        @pl.when(has_left)
        def _():
            copy(j, 0).wait_recv()
            copy(j, 3).wait_recv()

            @pl.when(d == 0)
            def _():
                left_in[j, 1, cz - 1 : cz, :] = (
                    left_in[j, 1, cz - 1 : cz, :] + rows_in[j, 1, last : last + 1, :]
                )

        @pl.when(has_right)
        def _():
            copy(j, 1).wait_recv()
            copy(j, 4).wait_recv()

            @pl.when(d == 1)
            def _():
                right_in[j, 1, PAD - 1 : PAD, :] = rows_in[j, 2, 2 * cx : 2 * cx + 1, :]

    below = pl.ds(PAD - 1, cz)
    above = pl.ds(PAD + 1, cz)

    def plane(j, x, shift):
        e0 = basis[j, 0, x, own, :]
        e1 = basis[j, 1, x, own, :]
        e2 = basis[j, 2, x, own, :]
        e0a = basis[j, 0, x, above, :]
        e1a = basis[j, 1, x, above, :]
        b1 = e1 - before(e1)
        b2 = e2 - basis[j, 2, x, below, :]
        if x == last:
            e1p = right_in[j, 0, own, :]
            e2p = right_in[j, 1, own, :]
            e2pb = right_in[j, 1, below, :]
        else:
            e1p = basis[j, 1, x + 1, own, :]
            e2p = basis[j, 2, x + 1, own, :]
            e2pb = basis[j, 2, x + 1, below, :]
        if x == 0:
            l1 = left_in[j, 0]
            l2 = left_in[j, 1]
        else:
            e0m = basis[j, 0, x - 1, own, :]
            l1 = basis[j, 1, x - 1, own, :] + (after(e0m) - e0m)
            l2 = basis[j, 2, x - 1, own, :] + (basis[j, 0, x - 1, above, :] - e0m)
        m = mass[x] + (4.0 - shift)
        g = (e1p - before(e1p)) + (e2p - e2pb) - (b1 + b2)
        q = b2 + e0
        o0 = m * e0 - (after(e0) + before(e0)) - (e0a + basis[j, 0, x, below, :]) + g
        o1 = m * e1 - (e1a + basis[j, 1, x, below, :]) - (e1p + l1) + (after(q) - q)
        o2 = (
            m * e2
            - (after(e2) + before(e2))
            - (e2p + l2)
            + ((e1a - before(e1a) + e0a) - (b1 + e0))
        )
        return o0, o1, o2

    def fold(f):
        return jnp.sum(f.reshape(cz // 8, 8, cy), axis=0)

    def finish(j, x, mode, sums):
        shift = 0.0 if mode == 0 else CENTRE
        outs = plane(j, x, shift)
        same, cross = sums
        for q in range(3):
            if mode == 0:
                new = -outs[q]
                if q == 0:
                    flat = ((s * cx + x) * (2 * cz) + z_start + row) * cy + lane
                    new = new + jnp.where(flat == cell_ref[0], SOURCE_AMP, 0.0)
            else:
                old = basis[j, q, x, own, :]
                if mode == 1:
                    new = (1.0 / HALF) * outs[q]
                else:
                    new = (2.0 / HALF) * outs[q] - basis[j - 1, q, x, own, :]
                cross = cross + fold(new * old)
            basis[j + 1, q, x, own, :] = new
            same = same + fold(new * new)
        return same, cross

    zero_sum = jnp.zeros((8, cy), jnp.float32)

    def step(j, mode, final):
        sums = (zero_sum, zero_sum)
        take_rows(j)
        for x in range(1, last):
            sums = finish(j, x, mode, sums)
        take_sides(j)
        sums = finish(j, last, mode, sums)
        if not final:
            send_right(j + 1)
        sums = finish(j, 0, mode, sums)
        if not final:
            send_left(j + 1)
            send_rows(j + 1)
        if mode == 0:
            dots[0] = sums[0]
        else:
            dots[2 * j - 1] = sums[1]
            dots[2 * j] = sums[0]

    load.wait()
    pl.semaphore_wait(barrier, group - 1 + n_src - 1)
    send_right(0)
    send_left(0)
    send_rows(0)
    step(0, 0, False)
    step(1, 1, False)

    def middle(j, carry):
        step(j, 2, False)
        return carry

    lax.fori_loop(2, DEGREE, middle, 0)
    step(DEGREE, 2, True)

    for k in range(2 * DEGREE + 1, 16):
        dots[k] = zero_sum
    mine = jnp.sum(dots[...], axis=1)
    dots_out[...] = mine

    def dot_copy(k):
        return pltpu.make_async_remote_copy(
            src_ref=dots_out,
            dst_ref=dots_in.at[k],
            send_sem=dot_send.at[k],
            recv_sem=dot_recv.at[k],
            device_id=member(k),
            device_id_type=MESH,
        )

    def dot_start(k, carry):
        dot_copy(k).start()
        return carry

    def dot_take(k, total):
        dot_copy(k).wait_recv()
        return total + dots_in[k]

    lax.fori_loop(1, group, dot_start, 0)
    total = lax.fori_loop(1, group, dot_take, mine)
    total = jnp.broadcast_to(jnp.sum(total, axis=1, keepdims=True), (16, cy))
    moments = [total[0:1]]
    for k in range(1, 2 * DEGREE + 1):
        if k % 2:
            value = total[k : k + 1]
            moments.append(value if k == 1 else 2.0 * value - moments[1])
        else:
            moments.append(2.0 * total[k : k + 1] - moments[0])
    coefficients = field_coefficients(moments)

    partial = []
    for x in range(cx):
        amount = None
        for q in range(3):
            value = basis[0, q, x, own, :]
            for k, weight in enumerate(coefficients):
                value = value + weight * basis[k + 1, q, x, own, :]
            out_ref[0, q, x] = value
            term = value * adj_ref[0, q, x]
            amount = term if amount is None else amount + term
        partial.append(amount)

    def packed(target):
        planes = []
        for a in range(cx // n_src):
            whole = None
            for b in range(n_src):
                moved = pltpu.roll(
                    partial[a * n_src + b], lax.rem((b - target + n_src) * share, cy), 1
                )
                keep = (lane >= b * share) & (lane < (b + 1) * share)
                whole = jnp.where(keep, moved, 0.0 if whole is None else whole)
            planes.append(whole)
        return planes

    def share_copy(k):
        return pltpu.make_async_remote_copy(
            src_ref=share_out.at[k],
            dst_ref=share_in.at[k],
            send_sem=share_send.at[k],
            recv_sem=share_recv.at[k],
            device_id=source(k),
            device_id_type=MESH,
        )

    for k in range(1, n_src):
        for a, value in enumerate(packed(lax.rem(c + k, n_src))):
            share_out[k, a] = value
        share_copy(k).start()
    summed = packed(c)
    for k in range(1, n_src):
        share_copy(k).wait_recv()
        summed = [value + share_in[k, a] for a, value in enumerate(summed)]
    for x in range(cx):
        a, b = divmod(x, n_src)
        scale = jnp.where(earth(x), -mass[x], 0.0)
        scale = pltpu.roll(scale, lax.rem((n_src - c) * share, cy), 1)
        value = summed[a] if b == 0 else pltpu.roll(summed[a], cy - b * share, 1)
        grad_ref[x] = (scale * value)[:, :share]

    def dot_drain(k, carry):
        dot_copy(k).wait_send()
        return carry

    lax.fori_loop(1, group, dot_drain, 0)
    for k in range(1, n_src):
        share_copy(k).wait_send()

    def drain(j, carry):
        copy(j, 2).wait_send()

        @pl.when(has_right)
        def _():
            copy(j, 0).wait_send()
            copy(j, 3).wait_send()

        @pl.when(has_left)
        def _():
            copy(j, 1).wait_send()
            copy(j, 4).wait_send()

        return carry

    lax.fori_loop(0, APPLIES, drain, 0)


def local(n_space, n_src, start_fields, adjoint_fields, conductivity, surface_rows, source_cells):
    _, _, cx, cz, cy = start_fields.shape
    group = n_space * 2
    f32 = jnp.float32
    vmem = pl.BlockSpec(memory_space=pltpu.VMEM)
    return pl.pallas_call(
        functools.partial(kernel, (n_space, n_src, cx, cz, cy)),
        out_shape=(
            jax.ShapeDtypeStruct(start_fields.shape, f32),
            jax.ShapeDtypeStruct((cx, cz, cy // n_src), f32),
        ),
        in_specs=[
            pl.BlockSpec(memory_space=pl.ANY),
            vmem,
            vmem,
            vmem,
            pl.BlockSpec(memory_space=pltpu.SMEM),
        ],
        out_specs=(vmem, vmem),
        scratch_shapes=[
            pltpu.VMEM((APPLIES + 1, 3, cx, cz + 2 * PAD, cy), f32),
            pltpu.VMEM((APPLIES, 2, cz + 2 * PAD, cy), f32),
            pltpu.VMEM((APPLIES, 2, cz, cy), f32),
            pltpu.VMEM((APPLIES, 2, cz, cy), f32),
            pltpu.VMEM((APPLIES, 16, cy), f32),
            pltpu.VMEM((APPLIES, 3, 16, cy), f32),
            pltpu.VMEM((cx, cz, cy), f32),
            pltpu.VMEM((16, 8, cy), f32),
            pltpu.VMEM((16, cy), f32),
            pltpu.VMEM((group, 16, cy), f32),
            pltpu.VMEM((n_src, cx // n_src, cz, cy), f32),
            pltpu.VMEM((n_src, cx // n_src, cz, cy), f32),
            pltpu.SemaphoreType.DMA,
            pltpu.SemaphoreType.DMA((APPLIES, 5)),
            pltpu.SemaphoreType.DMA((APPLIES, 5)),
            pltpu.SemaphoreType.DMA((group,)),
            pltpu.SemaphoreType.DMA((group,)),
            pltpu.SemaphoreType.DMA((n_src,)),
            pltpu.SemaphoreType.DMA((n_src,)),
        ],
        compiler_params=pltpu.CompilerParams(
            collective_id=0, has_side_effects=True, vmem_limit_bytes=40 * 1024 * 1024
        ),
    )(start_fields, adjoint_fields, conductivity, surface_rows, source_cells)


def solution(mesh):
    fields = P(("parts", "src"), None, "space", "depth", None)
    return jax.shard_map(
        functools.partial(local, mesh.shape["space"], mesh.shape["src"]),
        mesh=mesh,
        in_specs=(
            fields,
            fields,
            P(("parts", "space"), "depth", None),
            P(("parts", "space"), None),
            P(("parts", "src")),
        ),
        out_specs=(fields, P(("parts", "space"), "depth", "src")),
        check_vma=False,
    )
```

time: 270 us -> 46.6 us (0.17)
  blocking collectives: 115 us -> 0 us
  waiting for transfers between devices: 53.6 us -> 0 us
  starting transfers between devices: 42.2 us -> 0 us
  Pallas kernels: 0 us -> 40.1 us
  between operations: 30.6 us -> 1.3 us
  other arithmetic: 20.7 us -> 0 us
    psum x8 -> x0, blocking collectives: 115 us -> none  [the longest x3 43.2 us: local(): lax.psum((local_sum(t, s), local_sum(t, t)), ('space', 'depth'))]
    ppermute x28 -> x0, waiting for transfers between devices: 45 us -> none  [the longest x14 39.2 us: with_halo(): lax.ppermute(lax.slice_in_dim(block, 0, width, axis=dim), axis, backward)]
    ppermute x28 -> x0, starting transfers between devices: 42.2 us -> none  [the longest x14 23.9 us: with_halo(): lax.ppermute(lax.slice_in_dim(block, block.shape[dim] - width, None, axis...]
    pallas_call x0 -> x1, Pallas kernels: none -> 40.1 us  [local(): pl.pallas_call(functools.partial(kernel, (n_space, n_src, cx, cz, cy)), o...]
    reduce_sum x9 -> x0, other arithmetic: 8.63 us -> none  [the longest x8 6.48 us: local_sum(): return jnp.sum(left * right, axis=(1, 2, 3, 4))]
    unnamed x2 -> x0, waiting for transfers between devices: 8.52 us -> none
    concatenate x7 -> x0, other arithmetic: 3.44 us -> none  [with_halo(): block = jnp.concatenate([low, block, high], axis=dim)]
    sub x11 -> x0, other arithmetic: 3.36 us -> none  [the longest x7 1.84 us: curl_apply(): curl_z = fwd_x(e1) - fwd_y(e0)]
  transfers between devices with their start and end apart: 29 -> 0, of which waited for: 21 -> 0; matrix products, arithmetic and copies ran while one was open for 1% -> 0% of each run, Pallas kernels for 0% -> 0%
where the time goes in v1:
time: 46.6 us; the launch traced here: 46.3 us
  Pallas kernels  40.1 us (86%)
  local copies, waits for them, and re-layouts  4.97 us (11%)
  between operations  1.3 us (3%)
    pallas_call x1, Pallas kernels, local(): pl.pallas_call(functools.partial(kernel, (n_space, n_src, cx, cz, cy)), o...  40.1 us
    unnamed x10, local copies, waits for them, and re-layouts  4.97 us

profile of v1, /device:TPU:0, one launch (start us, length us, event | category | flops | bytes accessed | tf_op | source)
XLA Modules:
  0.0 46.3 jit_solution(14457999475795652853)
XLA Ops:
  1.3 0.0 copy-start
  1.3 1.0 %copy-done = f32[1,3,4,64,128]{4,3,2,1,0:T(8,128)S(1)} copy-done((f32[1,3,4,64,128]{4,3,2,1,0:T(8,128)S(1)}, f32[1,3,4,64,128]{4,3,2,1,0:T(8,128)}, u32[]{:S(2)}) %copy-start) | copy-done | bytes 393240
  2.3 0.0 copy-start.1
  2.3 1.0 %copy-done.1 = f32[1,3,4,64,128]{4,3,2,1,0:T(8,128)S(1)} copy-done((f32[1,3,4,64,128]{4,3,2,1,0:T(8,128)S(1)}, f32[1,3,4,64,128]{4,3,2,1,0:T(8,128)}, u32[]{:S(2)}) %copy-start.1) | copy-done | bytes 393240
  3.3 0.0 copy-start.2
  3.3 0.9 %copy-done.2 = f32[4,64,128]{2,1,0:T(8,128)S(1)} copy-done((f32[4,64,128]{2,1,0:T(8,128)S(1)}, f32[4,64,128]{2,1,0:T(8,128)}, u32[]{:S(2)}) %copy-start.2) | copy-done | bytes 131096
  4.2 0.0 copy-start.3
  4.2 0.7 %copy-done.3 = s32[4,128]{1,0:T(4,128)S(1)} copy-done((s32[4,128]{1,0:T(4,128)S(1)}, s32[4,128]{1,0:T(4,128)}, u32[]{:S(2)}) %copy-start.3) | copy-done | bytes 2072
  4.9 40.1 %shard_map.68 = (f32[1,3,4,64,128]{4,3,2,1,0:T(8,128)S(1)}, f32[4,64,64]{2,1,0:T(8,128)S(1)}) custom-call(f32[1,3,4,64,128]{4,3,2,1,0:T(8,128)S(1)} %copy-done, f32[1,3,4,64,128]{4,3,2,1,0:T(8,128)S(1)} %copy-done.1, f32[4,64,128]{2,1,0:T(8,128)S(1)} %copy-done.2, s32[4,128]{1,0:T(4,128)S(1)} %copy-done.3, s32[1]{0:T(128)S(6)} %copy.9.cell_ref), custom_call_target="tpu_custom_call" | custom-call | tf_op jit(solution)/shard_map/pallas_call | solution.py:488
  44.9 0.7 %copy.10 = f32[1,3,4,64,128]{4,3,2,1,0:T(8,128)} copy(f32[1,3,4,64,128]{4,3,2,1,0:T(8,128)S(1)} %get-tuple-element.4) | data formatting | bytes 786432
  45.7 0.7 %copy.11 = f32[4,64,64]{2,1,0:T(8,128)} copy(f32[4,64,64]{2,1,0:T(8,128)S(1)} %get-tuple-element.5) | data formatting | bytes 131072
Async XLA Ops:
  1.3 1.0 %copy-start = (f32[1,3,4,64,128]{4,3,2,1,0:T(8,128)S(1)}, f32[1,3,4,64,128]{4,3,2,1,0:T(8,128)}, u32[]{:S(2)}) copy-start(f32[1,3,4,64,128]{4,3,2,1,0:T(8,128)} %start_ref.1) | copy-start | bytes 1179652
  2.3 1.0 %copy-start.1 = (f32[1,3,4,64,128]{4,3,2,1,0:T(8,128)S(1)}, f32[1,3,4,64,128]{4,3,2,1,0:T(8,128)}, u32[]{:S(2)}) copy-start(f32[1,3,4,64,128]{4,3,2,1,0:T(8,128)} %adj_ref.1) | copy-start | bytes 1179652
  3.3 0.9 %copy-start.2 = (f32[4,64,128]{2,1,0:T(8,128)S(1)}, f32[4,64,128]{2,1,0:T(8,128)}, u32[]{:S(2)}) copy-start(f32[4,64,128]{2,1,0:T(8,128)} %cond_ref.1) | copy-start | bytes 393220
  4.2 0.7 %copy-start.3 = (s32[4,128]{1,0:T(4,128)S(1)}, s32[4,128]{1,0:T(4,128)}, u32[]{:S(2)}) copy-start(s32[4,128]{1,0:T(4,128)} %surf_ref.1) | copy-start | bytes 6148

commit v2 on v1

--- a/solution.py
+++ b/solution.py
@@ -103,9 +103,13 @@
     rows_out,
     rows_in,
     mass,
+    adj,
+    cond,
+    surf,
+    cell,
     dots,
-    dots_out,
     dots_in,
+    weights,
     share_out,
     share_in,
     load_sem,
@@ -118,33 +122,41 @@
 ):
     n_space, n_src, cx, cz, cy = sizes
     group = n_space * 2
+    everyone = group * n_src
     share = cy // n_src
     last = cx - 1
     s = lax.axis_index("space")
     d = lax.axis_index("depth")
     c = lax.axis_index("src")
-    me = s * 2 + d
-
-    def member(k):
-        g = lax.rem(me + k, group)
-        return {"space": g // 2, "depth": lax.rem(g, 2)}
+    me = c * group + s * 2 + d
+
+    def member(g):
+        return {"src": g // group, "space": lax.rem(g, group) // 2, "depth": lax.rem(g, 2)}
+
+    def other(k):
+        return lax.rem(me + k, everyone)
 
     def source(k):
         return {"src": lax.rem(c + k, n_src)}
 
+    own = pl.ds(PAD, cz)
+    load = pltpu.make_async_copy(start_ref.at[0], basis.at[0, :, :, own, :], load_sem.at[0])
+    load.start()
     barrier = pltpu.get_barrier_semaphore()
 
     def greet(k, carry):
-        pl.semaphore_signal(barrier, inc=1, device_id=member(k), device_id_type=MESH)
-        return carry
-
-    lax.fori_loop(1, group, greet, 0)
-    for k in range(1, n_src):
-        pl.semaphore_signal(barrier, inc=1, device_id=source(k), device_id_type=MESH)
-
-    own = pl.ds(PAD, cz)
-    load = pltpu.make_async_copy(start_ref.at[0], basis.at[0, :, :, own, :], load_sem)
-    load.start()
+        pl.semaphore_signal(barrier, inc=1, device_id=member(other(k)), device_id_type=MESH)
+        return carry
+
+    lax.fori_loop(1, everyone, greet, 0)
+    load_cond = pltpu.make_async_copy(cond_ref, cond, load_sem.at[1])
+    load_surf = pltpu.make_async_copy(surf_ref, surf, load_sem.at[2])
+    load_cell = pltpu.make_async_copy(cell_ref, cell, load_sem.at[3])
+    load_adj = pltpu.make_async_copy(adj_ref.at[0], adj, load_sem.at[4])
+    load_surf.start()
+    load_cond.start()
+    load_cell.start()
+    load_adj.start()
 
     lane = lax.broadcasted_iota(jnp.int32, (cz, cy), 1)
     row = lax.broadcasted_iota(jnp.int32, (cz, cy), 0)
@@ -154,10 +166,8 @@
     zero_row = jnp.zeros((1, cy), jnp.float32)
 
     def earth(x):
-        return (z_start + row) >= surf_ref[pl.ds(x, 1), :]
-
-    for x in range(cx):
-        mass[x] = ALPHA * jnp.where(earth(x), cond_ref[x], AIR)
+        return (z_start + row) >= surf[pl.ds(x, 1), :]
+
     zero_rows = jnp.zeros((3, cx, 1, cy), jnp.float32)
 
     def clear(j, carry):
@@ -249,11 +259,11 @@
             for x in range(cx):
                 basis[j, q, x, pl.ds(target, 1), :] = rows_in[j, 0, q * cx + x : q * cx + x + 1, :]
 
-    def take_sides(j):
+    def take_left(j):
         @pl.when(has_left)
         def _():
+            copy(j, 3).wait_recv()
             copy(j, 0).wait_recv()
-            copy(j, 3).wait_recv()
 
             @pl.when(d == 0)
             def _():
@@ -261,10 +271,11 @@
                     left_in[j, 1, cz - 1 : cz, :] + rows_in[j, 1, last : last + 1, :]
                 )
 
+    def take_right(j):
         @pl.when(has_right)
         def _():
+            copy(j, 4).wait_recv()
             copy(j, 1).wait_recv()
-            copy(j, 4).wait_recv()
 
             @pl.when(d == 1)
             def _():
@@ -321,7 +332,7 @@
                 new = -outs[q]
                 if q == 0:
                     flat = ((s * cx + x) * (2 * cz) + z_start + row) * cy + lane
-                    new = new + jnp.where(flat == cell_ref[0], SOURCE_AMP, 0.0)
+                    new = new + jnp.where(flat == cell[0], SOURCE_AMP, 0.0)
             else:
                 old = basis[j, q, x, own, :]
                 if mode == 1:
@@ -335,19 +346,61 @@
 
     zero_sum = jnp.zeros((8, cy), jnp.float32)
 
-    def step(j, mode, final):
+    def packed(planes, target):
+        out = []
+        for a in range(cx // n_src):
+            whole = None
+            for b in range(n_src):
+                moved = pltpu.roll(
+                    planes[a * n_src + b], lax.rem((b - target + n_src) * share, cy), 1
+                )
+                keep = (lane >= b * share) & (lane < (b + 1) * share)
+                whole = moved if b == 0 else jnp.where(keep, moved, whole)
+            out.append(whole)
+        return out
+
+    def share_copy(e, k):
+        return pltpu.make_async_remote_copy(
+            src_ref=share_out.at[e, k],
+            dst_ref=share_in.at[e, k],
+            send_sem=share_send.at[e, k],
+            recv_sem=share_recv.at[e, k],
+            device_id=source(k),
+            device_id_type=MESH,
+        )
+
+    def send_shares(e):
+        planes = []
+        for x in range(cx):
+            amount = basis[e, 0, x, own, :] * adj[0, x]
+            for q in range(1, 3):
+                amount = amount + basis[e, q, x, own, :] * adj[q, x]
+            planes.append(amount)
+        for k in range(n_src):
+            for a, value in enumerate(packed(planes, lax.rem(c + k, n_src))):
+                share_out[e, k, a] = value
+            if k:
+                share_copy(e, k).start()
+
+    def step(j, mode, final, right_first):
         sums = (zero_sum, zero_sum)
         take_rows(j)
         for x in range(1, last):
             sums = finish(j, x, mode, sums)
-        take_sides(j)
-        sums = finish(j, last, mode, sums)
+        for right in (right_first, not right_first):
+            if right:
+                take_right(j)
+                sums = finish(j, last, mode, sums)
+                if not final:
+                    send_right(j + 1)
+            else:
+                take_left(j)
+                sums = finish(j, 0, mode, sums)
+                if not final:
+                    send_left(j + 1)
         if not final:
-            send_right(j + 1)
-        sums = finish(j, 0, mode, sums)
-        if not final:
-            send_left(j + 1)
             send_rows(j + 1)
+            send_shares(j + 1)
         if mode == 0:
             dots[0] = sums[0]
         else:
@@ -355,98 +408,93 @@
             dots[2 * j] = sums[0]
 
     load.wait()
-    pl.semaphore_wait(barrier, group - 1 + n_src - 1)
+    pl.semaphore_wait(barrier, everyone - 1)
     send_right(0)
     send_left(0)
     send_rows(0)
-    step(0, 0, False)
-    step(1, 1, False)
-
-    def middle(j, carry):
-        step(j, 2, False)
-        return carry
-
-    lax.fori_loop(2, DEGREE, middle, 0)
-    step(DEGREE, 2, True)
-
-    for k in range(2 * DEGREE + 1, 16):
+    load_surf.wait()
+    load_cond.wait()
+    load_cell.wait()
+    for x in range(cx):
+        mass[x] = ALPHA * jnp.where(earth(x), cond[x], AIR)
+    load_adj.wait()
+    send_shares(0)
+    step(0, 0, False, False)
+    step(1, 1, False, True)
+
+    def middle(i, carry):
+        step(2 * i, 2, False, False)
+        step(2 * i + 1, 2, False, True)
+        return carry
+
+    lax.fori_loop(1, ITERS, middle, 0)
+    step(DEGREE, 2, True, False)
+
+    count = 2 * DEGREE + 1
+    for k in range(count, 16):
         dots[k] = zero_sum
-    mine = jnp.sum(dots[...], axis=1)
-    dots_out[...] = mine
-
-    def dot_copy(k):
+    mine = jnp.sum(jnp.sum(dots[...], axis=1), axis=1, keepdims=True)
+    diagonal = lax.broadcasted_iota(jnp.int32, (16, cy), 0) == lax.broadcasted_iota(
+        jnp.int32, (16, cy), 1
+    )
+    dots_in[me] = jnp.sum(jnp.where(diagonal, mine, 0.0), axis=0, keepdims=True)
+
+    def dot_copy(slot, k):
         return pltpu.make_async_remote_copy(
-            src_ref=dots_out,
-            dst_ref=dots_in.at[k],
+            src_ref=dots_in.at[slot],
+            dst_ref=dots_in.at[slot],
             send_sem=dot_send.at[k],
-            recv_sem=dot_recv.at[k],
-            device_id=member(k),
+            recv_sem=dot_recv.at[slot],
+            device_id=member(other(k)),
             device_id_type=MESH,
         )
 
     def dot_start(k, carry):
-        dot_copy(k).start()
-        return carry
-
-    def dot_take(k, total):
-        dot_copy(k).wait_recv()
-        return total + dots_in[k]
-
-    lax.fori_loop(1, group, dot_start, 0)
-    total = lax.fori_loop(1, group, dot_take, mine)
-    total = jnp.broadcast_to(jnp.sum(total, axis=1, keepdims=True), (16, cy))
-    moments = [total[0:1]]
-    for k in range(1, 2 * DEGREE + 1):
-        if k % 2:
-            value = total[k : k + 1]
-            moments.append(value if k == 1 else 2.0 * value - moments[1])
-        else:
-            moments.append(2.0 * total[k : k + 1] - moments[0])
-    coefficients = field_coefficients(moments)
-
-    partial = []
+        dot_copy(me, k).start()
+        return carry
+
+    def dot_take(k, carry):
+        dot_copy(other(k), k).wait_recv()
+        return carry
+
+    lax.fori_loop(1, everyone, dot_start, 0)
+    lax.fori_loop(1, everyone, dot_take, 0)
+    table = None
+    source_row = lax.broadcasted_iota(jnp.int32, (8, cy), 0)
+    for q in range(n_src):
+        total = dots_in[q * group]
+        for g in range(1, group):
+            total = total + dots_in[q * group + g]
+        total = jnp.broadcast_to(total, (8, cy))
+        table = total if q == 0 else jnp.where(source_row == q, total, table)
+    moments = []
+    for k in range(count):
+        value = jnp.broadcast_to(table[:, k : k + 1], (8, cy))
+        moments.append(value if k < 2 else 2.0 * value - moments[k % 2])
+    for k, value in enumerate(field_coefficients(moments)):
+        weights[k] = value
+
+    coefficients = [weights[k, pl.ds(c, 1), :] for k in range(DEGREE)]
     for x in range(cx):
-        amount = None
         for q in range(3):
             value = basis[0, q, x, own, :]
             for k, weight in enumerate(coefficients):
                 value = value + weight * basis[k + 1, q, x, own, :]
             out_ref[0, q, x] = value
-            term = value * adj_ref[0, q, x]
-            amount = term if amount is None else amount + term
-        partial.append(amount)
-
-    def packed(target):
-        planes = []
-        for a in range(cx // n_src):
-            whole = None
-            for b in range(n_src):
-                moved = pltpu.roll(
-                    partial[a * n_src + b], lax.rem((b - target + n_src) * share, cy), 1
-                )
-                keep = (lane >= b * share) & (lane < (b + 1) * share)
-                whole = jnp.where(keep, moved, 0.0 if whole is None else whole)
-            planes.append(whole)
-        return planes
-
-    def share_copy(k):
-        return pltpu.make_async_remote_copy(
-            src_ref=share_out.at[k],
-            dst_ref=share_in.at[k],
-            send_sem=share_send.at[k],
-            recv_sem=share_recv.at[k],
-            device_id=source(k),
-            device_id_type=MESH,
-        )
-
-    for k in range(1, n_src):
-        for a, value in enumerate(packed(lax.rem(c + k, n_src))):
-            share_out[k, a] = value
-        share_copy(k).start()
-    summed = packed(c)
-    for k in range(1, n_src):
-        share_copy(k).wait_recv()
-        summed = [value + share_in[k, a] for a, value in enumerate(summed)]
+    for e in range(DEGREE + 1):
+        for k in range(1, n_src):
+            share_copy(e, k).wait_recv()
+    summed = []
+    for a in range(cx // n_src):
+        value = None
+        for k in range(n_src):
+            origin = lax.rem(c + n_src - k, n_src)
+            held = share_in if k else share_out
+            term = held[0, k, a]
+            value = term if value is None else value + term
+            for e in range(DEGREE):
+                value = value + weights[e, pl.ds(origin, 1), :] * held[e + 1, k, a]
+        summed.append(value)
     for x in range(cx):
         a, b = divmod(x, n_src)
         scale = jnp.where(earth(x), -mass[x], 0.0)
@@ -455,12 +503,13 @@
         grad_ref[x] = (scale * value)[:, :share]
 
     def dot_drain(k, carry):
-        dot_copy(k).wait_send()
-        return carry
-
-    lax.fori_loop(1, group, dot_drain, 0)
-    for k in range(1, n_src):
-        share_copy(k).wait_send()
+        dot_copy(me, k).wait_send()
+        return carry
+
+    lax.fori_loop(1, everyone, dot_drain, 0)
+    for e in range(DEGREE + 1):
+        for k in range(1, n_src):
+            share_copy(e, k).wait_send()
 
     def drain(j, carry):
         copy(j, 2).wait_send()
@@ -482,22 +531,17 @@
 
 def local(n_space, n_src, start_fields, adjoint_fields, conductivity, surface_rows, source_cells):
     _, _, cx, cz, cy = start_fields.shape
-    group = n_space * 2
+    everyone = n_space * 2 * n_src
     f32 = jnp.float32
     vmem = pl.BlockSpec(memory_space=pltpu.VMEM)
+    shares = (DEGREE + 1, n_src, cx // n_src, cz, cy)
     return pl.pallas_call(
         functools.partial(kernel, (n_space, n_src, cx, cz, cy)),
         out_shape=(
             jax.ShapeDtypeStruct(start_fields.shape, f32),
             jax.ShapeDtypeStruct((cx, cz, cy // n_src), f32),
         ),
-        in_specs=[
-            pl.BlockSpec(memory_space=pl.ANY),
-            vmem,
-            vmem,
-            vmem,
-            pl.BlockSpec(memory_space=pltpu.SMEM),
-        ],
+        in_specs=[pl.BlockSpec(memory_space=pltpu.HBM)] * 5,
         out_specs=(vmem, vmem),
         scratch_shapes=[
             pltpu.VMEM((APPLIES + 1, 3, cx, cz + 2 * PAD, cy), f32),
@@ -507,18 +551,22 @@
             pltpu.VMEM((APPLIES, 16, cy), f32),
             pltpu.VMEM((APPLIES, 3, 16, cy), f32),
             pltpu.VMEM((cx, cz, cy), f32),
+            pltpu.VMEM((3, cx, cz, cy), f32),
+            pltpu.VMEM((cx, cz, cy), f32),
+            pltpu.VMEM((cx, cy), jnp.int32),
+            pltpu.SMEM((1,), jnp.int32),
             pltpu.VMEM((16, 8, cy), f32),
-            pltpu.VMEM((16, cy), f32),
-            pltpu.VMEM((group, 16, cy), f32),
-            pltpu.VMEM((n_src, cx // n_src, cz, cy), f32),
-            pltpu.VMEM((n_src, cx // n_src, cz, cy), f32),
-            pltpu.SemaphoreType.DMA,
+            pltpu.VMEM((everyone, 1, cy), f32),
+            pltpu.VMEM((DEGREE, 8, cy), f32),
+            pltpu.VMEM(shares, f32),
+            pltpu.VMEM(shares, f32),
+            pltpu.SemaphoreType.DMA((5,)),
             pltpu.SemaphoreType.DMA((APPLIES, 5)),
             pltpu.SemaphoreType.DMA((APPLIES, 5)),
-            pltpu.SemaphoreType.DMA((group,)),
-            pltpu.SemaphoreType.DMA((group,)),
-            pltpu.SemaphoreType.DMA((n_src,)),
-            pltpu.SemaphoreType.DMA((n_src,)),
+            pltpu.SemaphoreType.DMA((everyone,)),
+            pltpu.SemaphoreType.DMA((everyone,)),
+            pltpu.SemaphoreType.DMA((DEGREE + 1, n_src)),
+            pltpu.SemaphoreType.DMA((DEGREE + 1, n_src)),
         ],
         compiler_params=pltpu.CompilerParams(
             collective_id=0, has_side_effects=True, vmem_limit_bytes=40 * 1024 * 1024

time: 46.6 us -> 43.6 us (0.936)
  Pallas kernels: 40.1 us -> 37.1 us
    pallas_call x1, Pallas kernels: 40.1 us -> 37.1 us  [local(): pl.pallas_call(functools.partial(kernel, (n_space, n_src, cx, cz, cy)), o...]
where the time goes in v2:
time: 43.6 us; the launch traced here: 43.4 us
  Pallas kernels  37.1 us (85%)
  local copies, waits for them, and re-layouts  4.97 us (11%)
  between operations  1.3 us (3%)
    pallas_call x1, Pallas kernels, local(): pl.pallas_call(functools.partial(kernel, (n_space, n_src, cx, cz, cy)), o...  37.1 us
    unnamed x10, local copies, waits for them, and re-layouts  4.97 us

profile of v2, /device:TPU:0, one launch (start us, length us, event | category | flops | bytes accessed | tf_op | source)
XLA Modules:
  0.0 43.4 jit_solution(2903700453706768122)
XLA Ops:
  1.3 0.0 copy-start
  1.3 1.0 %copy-done = f32[1,3,4,64,128]{4,3,2,1,0:T(8,128)S(1)} copy-done((f32[1,3,4,64,128]{4,3,2,1,0:T(8,128)S(1)}, f32[1,3,4,64,128]{4,3,2,1,0:T(8,128)}, u32[]{:S(2)}) %copy-start) | copy-done | bytes 393240
  2.3 0.0 copy-start.1
  2.3 1.0 %copy-done.1 = f32[1,3,4,64,128]{4,3,2,1,0:T(8,128)S(1)} copy-done((f32[1,3,4,64,128]{4,3,2,1,0:T(8,128)S(1)}, f32[1,3,4,64,128]{4,3,2,1,0:T(8,128)}, u32[]{:S(2)}) %copy-start.1) | copy-done | bytes 393240
  3.3 0.0 copy-start.2
  3.3 0.9 %copy-done.2 = f32[4,64,128]{2,1,0:T(8,128)S(1)} copy-done((f32[4,64,128]{2,1,0:T(8,128)S(1)}, f32[4,64,128]{2,1,0:T(8,128)}, u32[]{:S(2)}) %copy-start.2) | copy-done | bytes 131096
  4.2 0.0 copy-start.3
  4.2 0.7 %copy-done.3 = s32[4,128]{1,0:T(4,128)S(1)} copy-done((s32[4,128]{1,0:T(4,128)S(1)}, s32[4,128]{1,0:T(4,128)}, u32[]{:S(2)}) %copy-start.3) | copy-done | bytes 2072
  4.9 37.1 %shard_map.68 = (f32[1,3,4,64,128]{4,3,2,1,0:T(8,128)S(1)}, f32[4,64,64]{2,1,0:T(8,128)S(1)}) custom-call(f32[1,3,4,64,128]{4,3,2,1,0:T(8,128)S(1)} %copy-done, f32[1,3,4,64,128]{4,3,2,1,0:T(8,128)S(1)} %copy-done.1, f32[4,64,128]{2,1,0:T(8,128)S(1)} %copy-done.2, s32[4,128]{1,0:T(4,128)S(1)} %copy-done.3, s32[1]{0:T(128)S(6)} %copy.9.cell_ref), custom_call_target="tpu_custom_call" | custom-call | tf_op jit(solution)/shard_map/pallas_call | solution.py:538
  42.0 0.7 %copy.10 = f32[1,3,4,64,128]{4,3,2,1,0:T(8,128)} copy(f32[1,3,4,64,128]{4,3,2,1,0:T(8,128)S(1)} %get-tuple-element.4) | data formatting | bytes 786432
  42.7 0.7 %copy.11 = f32[4,64,64]{2,1,0:T(8,128)} copy(f32[4,64,64]{2,1,0:T(8,128)S(1)} %get-tuple-element.5) | data formatting | bytes 131072
Async XLA Ops:
  1.3 1.0 %copy-start = (f32[1,3,4,64,128]{4,3,2,1,0:T(8,128)S(1)}, f32[1,3,4,64,128]{4,3,2,1,0:T(8,128)}, u32[]{:S(2)}) copy-start(f32[1,3,4,64,128]{4,3,2,1,0:T(8,128)} %start_ref.1) | copy-start | bytes 1179652
  2.3 1.0 %copy-start.1 = (f32[1,3,4,64,128]{4,3,2,1,0:T(8,128)S(1)}, f32[1,3,4,64,128]{4,3,2,1,0:T(8,128)}, u32[]{:S(2)}) copy-start(f32[1,3,4,64,128]{4,3,2,1,0:T(8,128)} %adj_ref.1) | copy-start | bytes 1179652
  3.3 0.9 %copy-start.2 = (f32[4,64,128]{2,1,0:T(8,128)S(1)}, f32[4,64,128]{2,1,0:T(8,128)}, u32[]{:S(2)}) copy-start(f32[4,64,128]{2,1,0:T(8,128)} %cond_ref.1) | copy-start | bytes 393220
  4.2 0.7 %copy-start.3 = (s32[4,128]{1,0:T(4,128)S(1)}, s32[4,128]{1,0:T(4,128)}, u32[]{:S(2)}) copy-start(s32[4,128]{1,0:T(4,128)} %surf_ref.1) | copy-start | bytes 6148

commit v3 on v2

--- a/solution.py
+++ b/solution.py
@@ -148,7 +148,24 @@
         pl.semaphore_signal(barrier, inc=1, device_id=member(other(k)), device_id_type=MESH)
         return carry
 
-    lax.fori_loop(1, everyone, greet, 0)
+    near_only = 2 <= n_space < DEGREE
+    if near_only:
+        for target in [{"depth": 1 - d}] + [source(k) for k in range(1, n_src)]:
+            pl.semaphore_signal(barrier, inc=1, device_id=target, device_id_type=MESH)
+        for present, side in ((s > 0, s - 1), (s < n_space - 1, s + 1)):
+
+            @pl.when(present)
+            def _():
+                for half in (d, 1 - d):
+                    pl.semaphore_signal(
+                        barrier,
+                        inc=1,
+                        device_id={"space": side, "depth": half},
+                        device_id_type=MESH,
+                    )
+
+    else:
+        lax.fori_loop(1, everyone, greet, 0)
     load_cond = pltpu.make_async_copy(cond_ref, cond, load_sem.at[1])
     load_surf = pltpu.make_async_copy(surf_ref, surf, load_sem.at[2])
     load_cell = pltpu.make_async_copy(cell_ref, cell, load_sem.at[3])
@@ -408,7 +425,19 @@
             dots[2 * j] = sums[0]
 
     load.wait()
-    pl.semaphore_wait(barrier, everyone - 1)
+    if near_only:
+        inside = has_left & has_right
+
+        @pl.when(inside)
+        def _():
+            pl.semaphore_wait(barrier, n_src + 4)
+
+        @pl.when(jnp.logical_not(inside))
+        def _():
+            pl.semaphore_wait(barrier, n_src + 2)
+
+    else:
+        pl.semaphore_wait(barrier, everyone - 1)
     send_right(0)
     send_left(0)
     send_rows(0)
@@ -457,6 +486,9 @@
         dot_copy(other(k), k).wait_recv()
         return carry
 
+    for e in range(DEGREE + 1):
+        for k in range(1, n_src):
+            share_copy(e, k).wait_recv()
     lax.fori_loop(1, everyone, dot_start, 0)
     lax.fori_loop(1, everyone, dot_take, 0)
     table = None
@@ -481,9 +513,6 @@
             for k, weight in enumerate(coefficients):
                 value = value + weight * basis[k + 1, q, x, own, :]
             out_ref[0, q, x] = value
-    for e in range(DEGREE + 1):
-        for k in range(1, n_src):
-            share_copy(e, k).wait_recv()
     summed = []
     for a in range(cx // n_src):
         value = None
@@ -569,7 +598,7 @@
             pltpu.SemaphoreType.DMA((DEGREE + 1, n_src)),
         ],
         compiler_params=pltpu.CompilerParams(
-            collective_id=0, has_side_effects=True, vmem_limit_bytes=40 * 1024 * 1024
+            collective_id=0, has_side_effects=True, vmem_limit_bytes=62 * 1024 * 1024
         ),
     )(start_fields, adjoint_fields, conductivity, surface_rows, source_cells)
 

time: 43.6 us -> 41.3 us (0.947)
  local copies, waits for them, and re-layouts: 4.97 us -> 2.46 us
    unnamed x10 -> x4, local copies, waits for them, and re-layouts: 4.97 us -> 2.46 us
where the time goes in v3:
time: 41.3 us; the launch traced here: 41.1 us
  Pallas kernels  37.4 us (91%)
  local copies, waits for them, and re-layouts  2.46 us (6%)
  between operations  1.29 us (3%)
    pallas_call x1, Pallas kernels, local(): pl.pallas_call(functools.partial(kernel, (n_space, n_src, cx, cz, cy)), o...  37.4 us
    unnamed x4, local copies, waits for them, and re-layouts  2.46 us

profile of v3, /device:TPU:0, one launch (start us, length us, event | category | flops | bytes accessed | tf_op | source)
XLA Modules:
  0.0 41.1 jit_solution(8171999556182939082)
XLA Ops:
  1.3 37.4 %shard_map.68 = (f32[1,3,4,64,128]{4,3,2,1,0:T(8,128)}, f32[4,64,64]{2,1,0:T(8,128)}) custom-call(f32[1,3,4,64,128]{4,3,2,1,0:T(8,128)} %start_ref.1, f32[1,3,4,64,128]{4,3,2,1,0:T(8,128)} %adj_ref.1, f32[4,64,128]{2,1,0:T(8,128)} %cond_ref.1, s32[4,128]{1,0:T(4,128)} %surf_ref.1, s32[1]{0:T(128)S(6)} %copy.9.cell_ref), custom_call_target="tpu_custom_call" | custom-call | tf_op jit(solution)/shard_map/pallas_call | solution.py:567
  38.7 0.0 copy-start
  38.7 1.8 %copy.10 = f32[1,3,4,64,128]{4,3,2,1,0:T(8,128)} copy(f32[1,3,4,64,128]{4,3,2,1,0:T(8,128)} %get-tuple-element.4) | data formatting | bytes 786432
  40.5 0.0 copy-done
  40.5 0.7 %copy.11 = f32[4,64,64]{2,1,0:T(8,128)} copy(f32[4,64,64]{2,1,0:T(8,128)S(1)} %copy-done) | data formatting | bytes 131072
Async XLA Ops:
  38.7 1.8 %copy-start = (f32[4,64,64]{2,1,0:T(8,128)S(1)}, f32[4,64,64]{2,1,0:T(8,128)}, u32[]{:S(2)}) copy-start(f32[4,64,64]{2,1,0:T(8,128)} %get-tuple-element.5) | copy-start | bytes 196612

commit v4 on v3

--- a/solution.py
+++ b/solution.py
@@ -102,6 +102,8 @@
     left_out,
     rows_out,
     rows_in,
+    edge_out,
+    edge_in,
     mass,
     adj,
     cond,
@@ -221,12 +223,12 @@
             src = basis.at[j, pl.ds(1, 2), 0, own, :]
             dst, where = right_in.at[j, :, own, :], {"space": s - 1}
         else:
-            src, dst = rows_out.at[j], rows_in.at[j, kind - 2]
             where = {"depth": 1 - d}
-            if kind == 3:
-                where["space"] = s + 1
-            elif kind == 4:
-                where["space"] = s - 1
+            if kind == 2:
+                src, dst = rows_out.at[j], rows_in.at[j]
+            else:
+                src, dst = edge_out.at[j, kind - 3], edge_in.at[j, kind - 3]
+                where["space"] = s + 1 if kind == 3 else s - 1
         return pltpu.make_async_remote_copy(
             src_ref=src,
             dst_ref=dst,
@@ -239,7 +241,15 @@
     has_left = s > 0
     has_right = s < n_space - 1
 
+    edge = PAD + (cz - 1) * (1 - d)
+
     def send_right(j):
+        edge_out[j, 0] = jnp.broadcast_to(basis[j, 0, last, pl.ds(edge, 1), :], (8, cy))
+
+        @pl.when(has_right)
+        def _():
+            copy(j, 3).start()
+
         e0 = basis[j, 0, last, own, :]
         left_out[j, 0] = basis[j, 1, last, own, :] + after(e0) - e0
         left_out[j, 1] = basis[j, 2, last, own, :] + basis[j, 0, last, pl.ds(PAD + 1, cz), :] - e0
@@ -249,11 +259,12 @@
             copy(j, 0).start()
 
     def send_left(j):
+        edge_out[j, 1] = jnp.broadcast_to(basis[j, 2, 0, pl.ds(edge, 1), :], (8, cy))
+
         @pl.when(has_left)
         def _():
+            copy(j, 4).start()
             copy(j, 1).start()
-
-    edge = PAD + (cz - 1) * (1 - d)
 
     def send_rows(j):
         for q in range(3):
@@ -261,20 +272,12 @@
                 rows_out[j, q * cx + x : q * cx + x + 1, :] = basis[j, q, x, pl.ds(edge, 1), :]
         copy(j, 2).start()
 
-        @pl.when(has_right)
-        def _():
-            copy(j, 3).start()
-
-        @pl.when(has_left)
-        def _():
-            copy(j, 4).start()
-
     def take_rows(j):
         copy(j, 2).wait_recv()
         target = PAD - 1 + (cz + 1) * (1 - d)
         for q in range(3):
             for x in range(cx):
-                basis[j, q, x, pl.ds(target, 1), :] = rows_in[j, 0, q * cx + x : q * cx + x + 1, :]
+                basis[j, q, x, pl.ds(target, 1), :] = rows_in[j, q * cx + x : q * cx + x + 1, :]
 
     def take_left(j):
         @pl.when(has_left)
@@ -285,7 +288,7 @@
             @pl.when(d == 0)
             def _():
                 left_in[j, 1, cz - 1 : cz, :] = (
-                    left_in[j, 1, cz - 1 : cz, :] + rows_in[j, 1, last : last + 1, :]
+                    left_in[j, 1, cz - 1 : cz, :] + edge_in[j, 0, 0:1, :]
                 )
 
     def take_right(j):
@@ -296,7 +299,7 @@
 
             @pl.when(d == 1)
             def _():
-                right_in[j, 1, PAD - 1 : PAD, :] = rows_in[j, 2, 2 * cx : 2 * cx + 1, :]
+                right_in[j, 1, PAD - 1 : PAD, :] = edge_in[j, 1, 0:1, :]
 
     below = pl.ds(PAD - 1, cz)
     above = pl.ds(PAD + 1, cz)
@@ -578,7 +581,9 @@
             pltpu.VMEM((APPLIES, 2, cz, cy), f32),
             pltpu.VMEM((APPLIES, 2, cz, cy), f32),
             pltpu.VMEM((APPLIES, 16, cy), f32),
-            pltpu.VMEM((APPLIES, 3, 16, cy), f32),
+            pltpu.VMEM((APPLIES, 16, cy), f32),
+            pltpu.VMEM((APPLIES, 2, 8, cy), f32),
+            pltpu.VMEM((APPLIES, 2, 8, cy), f32),
             pltpu.VMEM((cx, cz, cy), f32),
             pltpu.VMEM((3, cx, cz, cy), f32),
             pltpu.VMEM((cx, cz, cy), f32),

time: 41.3 us -> 40 us (0.969)
  Pallas kernels: 37.4 us -> 36.1 us
    pallas_call x1, Pallas kernels: 37.4 us -> 36.1 us  [local(): pl.pallas_call(functools.partial(kernel, (n_space, n_src, cx, cz, cy)), o...]
where the time goes in v4:
time: 40 us; the launch traced here: 39.8 us
  Pallas kernels  36.1 us (90%)
  local copies, waits for them, and re-layouts  2.46 us (6%)
  between operations  1.29 us (3%)
    pallas_call x1, Pallas kernels, local(): pl.pallas_call(functools.partial(kernel, (n_space, n_src, cx, cz, cy)), o...  36.1 us
    unnamed x4, local copies, waits for them, and re-layouts  2.46 us

profile of v4, /device:TPU:0, one launch (start us, length us, event | category | flops | bytes accessed | tf_op | source)
XLA Modules:
  0.0 39.8 jit_solution(4973656588002775913)
XLA Ops:
  1.3 36.1 %shard_map.68 = (f32[1,3,4,64,128]{4,3,2,1,0:T(8,128)}, f32[4,64,64]{2,1,0:T(8,128)}) custom-call(f32[1,3,4,64,128]{4,3,2,1,0:T(8,128)} %start_ref.1, f32[1,3,4,64,128]{4,3,2,1,0:T(8,128)} %adj_ref.1, f32[4,64,128]{2,1,0:T(8,128)} %cond_ref.1, s32[4,128]{1,0:T(4,128)} %surf_ref.1, s32[1]{0:T(128)S(6)} %copy.9.cell_ref), custom_call_target="tpu_custom_call" | custom-call | tf_op jit(solution)/shard_map/pallas_call | solution.py:570
  37.4 0.0 copy-start
  37.4 1.8 %copy.10 = f32[1,3,4,64,128]{4,3,2,1,0:T(8,128)} copy(f32[1,3,4,64,128]{4,3,2,1,0:T(8,128)} %get-tuple-element.4) | data formatting | bytes 786432
  39.2 0.0 copy-done
  39.2 0.7 %copy.11 = f32[4,64,64]{2,1,0:T(8,128)} copy(f32[4,64,64]{2,1,0:T(8,128)S(1)} %copy-done) | data formatting | bytes 131072
Async XLA Ops:
  37.4 1.8 %copy-start = (f32[4,64,64]{2,1,0:T(8,128)S(1)}, f32[4,64,64]{2,1,0:T(8,128)}, u32[]{:S(2)}) copy-start(f32[4,64,64]{2,1,0:T(8,128)} %get-tuple-element.5) | copy-start | bytes 196612
